TPU v7x, 32 devices: a whole 2x2x4 slice. The times are simulated.
32 devices in a mesh: col: 4 (over y, x), af: 8 (over z, core).
Axes of the slice: x: 2, y: 2, z: 4, core: 2. Of those that a mesh axis runs over, the one named last changes fastest.
Arguments:
- inputs: bfloat16 [2, 64, 64, 8, 256], P(None, 'col', 'af'), may hold values from -6 to 6
- first_filters: bfloat16 [3, 3, 3, 256, 256], P(None, None, None, 'af'), may hold values from -0.109375 to 0.109375
- second_filters: bfloat16 [3, 3, 3, 256, 256], P(None, None, None, 'af'), may hold values from -0.125 to 0.125
Outputs:
- features: bfloat16 [2, 32, 32, 4, 256], P(None, 'col', None, None, 'af')
All inputs are finite; a program needn't handle non-finite values.
Results may differ from a plain program's by a relative error of at most 0.011.
Values may be sent and summed in bfloat16 or wider, within the bound.
A program may use at most 64 MiB of HBM per device.

v0:
```python
import jax
import jax.numpy as jnp
from jax import lax
from jax.sharding import PartitionSpec as P


def extended(block, sides, width):
    for axis, dim in sides:
        count = lax.axis_size(axis)
        forward = [(i, i + 1) for i in range(count - 1)]
        backward = [(target, source) for source, target in forward]
        low = lax.ppermute(
            lax.slice_in_dim(block, block.shape[dim] - width, None, axis=dim), axis, forward
        )
        high = lax.ppermute(lax.slice_in_dim(block, 0, width, axis=dim), axis, backward)
        block = jnp.concatenate([low, block, high], axis=dim)
    return block


def passed_along(array, axis, by):
    peers = lax.axis_size(axis)
    pairs = [(i, i + by) for i in range(peers) if 0 <= i + by < peers]
    return lax.ppermute(array, axis, pairs)


def convolve(volume, kernel, stride, row_pad):
    return lax.conv_general_dilated(
        volume,
        kernel,
        (stride, stride, stride),
        ((0, 0), (row_pad, row_pad), (1, 1)),
        dimension_numbers=("NDHWC", "DHWIO", "NDHWC"),
        preferred_element_type=jnp.float32,
    )


def per_device(inputs, first_filters, second_filters):
    padded = extended(inputs, (("col", 1),), 1)
    gathered = lax.all_gather(padded, "af", axis=2, tiled=True)
    own_first = lax.all_to_all(first_filters, "af", split_axis=4, concat_axis=3, tiled=True)
    hidden = jnp.maximum(convolve(gathered, own_first, 1, 1), 0.0).astype(jnp.bfloat16)
    lower_plane = passed_along(hidden[:, -1:], "col", 1)
    stacked = jnp.concatenate([lower_plane, hidden], axis=1)
    all_channels = lax.all_gather(stacked, "af", axis=4, tiled=True)
    own_second = lax.all_to_all(second_filters, "af", split_axis=4, concat_axis=3, tiled=True)
    totals = convolve(all_channels, own_second, 2, 1)
    return jnp.maximum(totals, 0.0).astype(jnp.bfloat16)


def solution(mesh):
    placed = (
        P(None, "col", "af", None, None),
        P(None, None, None, "af", None),
        P(None, None, None, "af", None),
    )
    return jax.shard_map(
        per_device,
        mesh=mesh,
        in_specs=placed,
        out_specs=P(None, "col", None, None, "af"),
        check_vma=False,
    )
```

profile of v0, /device:TPU:0, one launch (start us, length us, event | category | flops | bytes accessed | tf_op | source)
XLA Modules:
  0.0 505.1 jit_solution(15341634197344286966)
XLA Ops:
  6.5 0.0 copy-start.1
  6.5 0.0 all-gather.3.cloned.1.call-start
  6.5 2.9 copy.20
  9.4 0.1 fusion.1
  9.6 4.8 collective-permute-start
  14.4 1.3 collective-permute-start.1
  15.7 0.6 collective-permute-done
  16.3 4.3 collective-permute-done.1
  20.6 2.6 pad_maximum_fusion.1
  23.2 0.0 all-gather.3.cloned.1.call-update
  23.2 0.0 all-gather.5.cloned.1.call-start
  23.3 0.0 copy-done.1
  23.3 1.9 copy.23
  25.2 1.7 reshape
  26.9 28.6 %all_to_all.36 = bf16[8,2,13824]{2,1,0:T(2,128)(2,1)S(1)} all-to-all(bf16[8,2,13824]{2,1,0:T(2,128)(2,1)S(1)} %reshape), channel_id=1, replica_groups=mesh['col'=4,'af'=8] {'af'}, dimensions={0} | all-to-all | bytes 884736 | tf_op jit(solution)/shard_map/all_to_all | solution.py:40
  55.5 1.5 reshape.1
  57.0 2.7 copy.37
  59.7 2.8 all_to_all.29
  62.4 60.6 %all-gather.3.cloned.1.call-done = bf16[2,18,64,8,256]{4,0,3,2,1:T(2,128)(2,1)} async-done(((bf16[2,18,8,8,256]{4,0,3,2,1:T(2,128)(2,1)}), bf16[2,18,64,8,256]{4,0,3,2,1:T(2,128)(2,1)}) %all-gather.3.cloned.1.call-update) | async-done | bytes 9437200 | tf_op jit(solution)/shard_map/all_gather | solution.py:39
  123.0 119.1 %maximum_convert_fusion = bf16[2,16,64,8,32]{4,0,3,2,1:T(2,128)(2,1)S(1)} fusion(bf16[2,18,64,8,256]{4,0,3,2,1:T(2,128)(2,1)} %all-gather.3.cloned.1.call-done, bf16[3,3,3,256,32]{3,4,2,1,0:T(8,128)(2,1)S(1)} %all_to_all.29), kind=kOutput, calls=%fused_computation | convolution fusion | flops 6575620096 | bytes 10928128 | tf_op jit(solution)/shard_map/conv_general_dilated | solution.py:27
  242.2 0.0 copy-start
  242.2 2.0 copy-done
  244.2 0.2 slice.14
  244.4 4.3 collective-permute-start.2
  248.7 5.9 %collective-permute-done.2 = bf16[2,1,64,8,32]{4,0,3,2,1:T(2,128)(2,1)S(1)} collective-permute-done((bf16[2,1,64,8,32]{4,0,3,2,1:T(2,128)(2,1)S(1)}, bf16[2,1,64,8,32]{4,0,3,2,1:T(2,128)(2,1)S(1)}, u32[]{:S(2)}, u32[]{:S(2)}) %collective-permute-start.2) | collective-permute-done | bytes 65568 | tf_op jit(solution)/shard_map/ppermute | solution.py:23
  254.7 11.1 %pad_maximum_fusion = bf16[2,17,64,8,32]{4,0,3,2,1:T(2,128)(2,1)} fusion(bf16[2,16,64,8,32]{4,0,3,2,1:T(2,128)(2,1)} %copy-done, bf16[2,1,64,8,32]{4,0,3,2,1:T(2,128)(2,1)S(1)} %collective-permute-done.2), kind=kLoop, calls=%fused_computation.1 | loop fusion | flops 557056 | bytes 2228224 | tf_op jit(solution)/shard_map/concatenate | solution.py:43
  265.8 0.0 copy-start.2
  265.8 12.6 %copy.25 = bf16[2,17,64,8,32]{2,3,1,0,4:T(8,128)(2,1)} copy(bf16[2,17,64,8,32]{4,0,3,2,1:T(2,128)(2,1)} %pad_maximum_fusion) | data formatting | bytes 2228224 | tf_op jit(solution)/shard_map/concatenate | solution.py:43
  278.4 0.0 all-gather.5.cloned.1.call-update
  278.4 0.0 copy-done.2
  278.4 1.9 copy.26
  280.3 1.7 reshape.2
  282.0 24.8 %all_to_all.37 = bf16[8,2,13824]{2,1,0:T(2,128)(2,1)S(1)} all-to-all(bf16[8,2,13824]{2,1,0:T(2,128)(2,1)S(1)} %reshape.2), channel_id=1, replica_groups=mesh['col'=4,'af'=8] {'af'}, dimensions={0} | all-to-all | bytes 884736 | tf_op jit(solution)/shard_map/all_to_all | solution.py:45
  306.8 1.5 reshape.3
  308.3 2.7 copy.36
  311.1 2.8 all_to_all.33
  313.8 129.7 %all-gather.5.cloned.1.call-done = bf16[2,17,64,8,256]{2,3,1,0,4:T(8,128)(2,1)} async-done(((bf16[2,17,64,8,32]{2,3,1,0,4:T(8,128)(2,1)}), bf16[2,17,64,8,256]{2,3,1,0,4:T(8,128)(2,1)}) %all-gather.5.cloned.1.call-update) | async-done | bytes 8912912 | tf_op jit(solution)/shard_map/all_gather | solution.py:44
  443.6 31.0 %copy.28 = bf16[2,17,64,8,256]{4,0,3,2,1:T(2,128)(2,1)} copy(bf16[2,17,64,8,256]{2,3,1,0,4:T(8,128)(2,1)} %all-gather.5.cloned.1.call-done) | data formatting | bytes 17825792 | tf_op jit(solution)/shard_map/all_gather | solution.py:44
  474.5 22.3 %fusion.2 = bf16[2,8,32,4,32]{4,0,3,2,1:T(2,128)(2,1)S(1)} fusion(bf16[2,17,64,8,256]{4,0,3,2,1:T(2,128)(2,1)} %copy.28, bf16[3,3,3,256,32]{3,4,2,1,0:T(8,128)(2,1)S(1)} %all_to_all.33), kind=kOutput, calls=%fused_computation.8 | convolution fusion | flops 821821440 | bytes 9486336 | tf_op jit(solution)/shard_map/conv_general_dilated | solution.py:27
  496.8 0.1 fusion
  496.9 1.1 copy.30
Async XLA Ops:
  6.5 16.8 %copy-start.1 = (bf16[3,3,3,32,256]{4,3,2,1,0:T(8,128)(2,1)S(1)}, bf16[3,3,3,32,256]{4,3,2,1,0:T(8,128)(2,1)}, u32[]{:S(2)}) copy-start(bf16[3,3,3,32,256]{4,3,2,1,0:T(8,128)(2,1)} %param.4) | copy-start | bytes 1327108
  6.5 116.5 %all-gather.3.cloned.1.call-start = ((), (), s32[]{:S(2)}) async-start(), calls=%async_computation.2 | async-start | bytes 10616832 | tf_op jit(solution)/shard_map/all_gather | solution.py:39
  9.6 6.7 %collective-permute-start = (bf16[2,1,8,8,256]{4,0,3,2,1:T(2,128)(2,1)S(1)}, bf16[2,1,8,8,256]{4,0,3,2,1:T(2,128)(2,1)S(1)}, u32[]{:S(2)}, u32[]{:S(2)}) collective-permute-start(bf16[2,1,8,8,256]{4,0,3,2,1:T(2,128)(2,1)S(1)} %get-tuple-element.5), channel_id=1, source_target_pairs={{0,8},{8,16},{16,24},{1,9},{9,17},{17,25},{2,10},{10,18},{18,26},{... | collective-permute-start | bytes 196616 | tf_op jit(solution)/shard_map/ppermute | solution.py:12
  14.4 6.2 %collective-permute-start.1 = (bf16[2,1,8,8,256]{4,0,3,2,1:T(2,128)(2,1)S(1)}, bf16[2,1,8,8,256]{4,0,3,2,1:T(2,128)(2,1)S(1)}, u32[]{:S(2)}, u32[]{:S(2)}) collective-permute-start(bf16[2,1,8,8,256]{4,0,3,2,1:T(2,128)(2,1)S(1)} %get-tuple-element.6), channel_id=1, source_target_pairs={{8,0},{16,8},{24,16},{9,1},{17,9},{25,17},{10,2},{18,10},{26,18},{... | collective-permute-start | bytes 196616 | tf_op jit(solution)/shard_map/ppermute | solution.py:15
  23.2 420.3 %all-gather.5.cloned.1.call-start = ((), (), s32[]{:S(2)}) async-start(), calls=%async_computation.3 | async-start | bytes 20054016 | tf_op jit(solution)/shard_map/all_gather | solution.py:44
  242.2 2.0 copy-start
  244.4 10.3 %collective-permute-start.2 = (bf16[2,1,64,8,32]{4,0,3,2,1:T(2,128)(2,1)S(1)}, bf16[2,1,64,8,32]{4,0,3,2,1:T(2,128)(2,1)S(1)}, u32[]{:S(2)}, u32[]{:S(2)}) collective-permute-start(bf16[2,1,64,8,32]{4,0,3,2,1:T(2,128)(2,1)S(1)} %slice.14), channel_id=1, source_target_pairs={{0,8},{8,16},{16,24},{1,9},{9,17},{17,25},{2,10},{10,18},{18,26},{... | collective-permute-start | bytes 196616 | tf_op jit(solution)/shard_map/ppermute | solution.py:23
  265.8 12.6 %copy-start.2 = (bf16[3,3,3,32,256]{4,3,2,1,0:T(8,128)(2,1)S(1)}, bf16[3,3,3,32,256]{4,3,2,1,0:T(8,128)(2,1)}, u32[]{:S(2)}) copy-start(bf16[3,3,3,32,256]{4,3,2,1,0:T(8,128)(2,1)} %param.5) | copy-start | bytes 1327108
Sparse Core Ops, SparseCore 0:
  23.4 99.6 all-gather.2
  278.5 165.0 all-gather.4
where the time goes:
time: 512 us; the launch traced here: 505 us
  waiting for transfers between devices  201 us (39%)
  matrix products  141 us (28%)
  local copies, waits for them, and re-layouts  71 us (14%)
  blocking collectives  53.4 us (10%)
  other arithmetic  13.9 us (3%)
  between operations  13.8 us (3%)
  starting transfers between devices  10.5 us (2%)
    conv_general_dilated x2, matrix products, convolve(): lax.conv_general_dilated(volume, kernel, (stride, stride, stride), ((0, 0...  141 us
    all_gather x1, waiting for transfers between devices, per_device(): all_channels = lax.all_gather(stacked, 'af', axis=4, tiled=True)  130 us
    all_gather x1, waiting for transfers between devices, per_device(): gathered = lax.all_gather(padded, 'af', axis=2, tiled=True)  60.6 us
    all_gather x1, local copies, waits for them, and re-layouts, per_device(): all_channels = lax.all_gather(stacked, 'af', axis=4, tiled=True)  31 us
    all_to_all x1, blocking collectives, per_device(): lax.all_to_all(first_filters, 'af', split_axis=4, concat_axis=3, tiled=True)  28.6 us
    all_to_all x1, blocking collectives, per_device(): lax.all_to_all(second_filters, 'af', split_axis=4, concat_axis=3, tiled=T...  24.8 us
    unnamed x13, local copies, waits for them, and re-layouts  15.2 us
    concatenate x1, local copies, waits for them, and re-layouts, per_device(): stacked = jnp.concatenate([lower_plane, hidden], axis=1)  12.6 us
  transfers between devices with their start and end apart: 5, of which 5 were waited for; matrix products, arithmetic and copies ran while one was open for 3% of the time, Pallas kernels for 0%

commit v1 on v0

v1 whole, which is shorter than its diff:
```python
import jax
import jax.numpy as jnp
from jax import lax
from jax.sharding import PartitionSpec as P


def extended(block, axis, dim, low_width, high_width):
    count = lax.axis_size(axis)
    forward = [(i, i + 1) for i in range(count - 1)]
    backward = [(target, source) for source, target in forward]
    size = block.shape[dim]
    low = lax.ppermute(
        lax.slice_in_dim(block, size - low_width, None, axis=dim), axis, forward
    )
    high = lax.ppermute(lax.slice_in_dim(block, 0, high_width, axis=dim), axis, backward)
    return jnp.concatenate([low, block, high], axis=dim)


def convolve(volume, kernel, stride):
    return lax.conv_general_dilated(
        volume,
        kernel,
        (stride, stride, stride),
        ((0, 0), (0, 0), (1, 1)),
        dimension_numbers=("NDHWC", "DHWIO", "NDHWC"),
        preferred_element_type=jnp.float32,
    )


def per_device(inputs, first_filters, second_filters):
    first = lax.all_gather(first_filters, "af", axis=3, tiled=True)
    second = lax.all_gather(second_filters, "af", axis=3, tiled=True)
    block = extended(inputs, "col", 1, 2, 1)
    block = extended(block, "af", 2, 2, 1)
    hidden = jnp.maximum(convolve(block, first, 1), 0.0).astype(jnp.bfloat16)
    planes = lax.broadcasted_iota(jnp.int32, (1, hidden.shape[1], 1, 1, 1), 1)
    rows = lax.broadcasted_iota(jnp.int32, (1, 1, hidden.shape[2], 1, 1), 2)
    inside = (planes + lax.axis_index("col") > 0) & (rows + lax.axis_index("af") > 0)
    hidden = jnp.where(inside, hidden, jnp.zeros_like(hidden))
    features = jnp.maximum(convolve(hidden, second, 2), 0.0).astype(jnp.bfloat16)
    return lax.all_to_all(features, "af", split_axis=4, concat_axis=2, tiled=True)


def solution(mesh):
    placed = (
        P(None, "col", "af", None, None),
        P(None, None, None, "af", None),
        P(None, None, None, "af", None),
    )
    return jax.shard_map(
        per_device,
        mesh=mesh,
        in_specs=placed,
        out_specs=P(None, "col", None, None, "af"),
        check_vma=False,
    )
```

time: 512 us -> 130 us (0.25); the launches traced: 505 us -> 130 us
  waiting for transfers between devices: 201 us -> 51 us
  matrix products: 141 us -> 33.3 us
  local copies, waits for them, and re-layouts: 71 us -> 13.6 us
  blocking collectives: 53.4 us -> 9.29 us
  other arithmetic: 13.9 us -> 0.17 us
    all_gather x2, waiting for transfers between devices: 190 us -> 42.9 us  [the longest x1 27 us: per_device(): first = lax.all_gather(first_filters, 'af', axis=3, tiled=True)]
    conv_general_dilated x2, matrix products: 141 us -> 33.3 us  [convolve(): lax.conv_general_dilated(volume, kernel, (stride, stride, stride), ((0, 0...]
    all_to_all x2 -> x1, blocking collectives: 53.4 us -> 9.29 us  [per_device(): lax.all_to_all(features, 'af', split_axis=4, concat_axis=2, tiled=True)]
    all_gather x1 -> x0, local copies, waits for them, and re-layouts: 31 us -> none  [per_device(): all_channels = lax.all_gather(stacked, 'af', axis=4, tiled=True)]
    concatenate x2 -> x0, other arithmetic: 13.7 us -> none  [the longest x1 11.1 us: per_device(): stacked = jnp.concatenate([lower_plane, hidden], axis=1)]
    concatenate x1, local copies, waits for them, and re-layouts: 12.6 us -> 0.06 us  [extended(): return jnp.concatenate([low, block, high], axis=dim)]
    unnamed x13 -> x8, local copies, waits for them, and re-layouts: 15.2 us -> 6.65 us
    all_to_all x4 -> x1, local copies, waits for them, and re-layouts: 10.9 us -> 2.96 us  [per_device(): lax.all_to_all(features, 'af', split_axis=4, concat_axis=2, tiled=True)]
  transfers between devices with their start and end apart: 5 -> 6, of which waited for: 5 -> 5; matrix products, arithmetic and copies ran while one was open for 3% -> 25% of each run, Pallas kernels for 0% -> 0%
where the time goes in v1:
time: 130 us
  waiting for transfers between devices  51 us (39%)
  matrix products  33.3 us (26%)
  local copies, waits for them, and re-layouts  13.6 us (10%)
  between operations  13.5 us (10%)
  blocking collectives  9.29 us (7%)
  starting transfers between devices  8.78 us (7%)
    conv_general_dilated x2, matrix products, convolve(): lax.conv_general_dilated(volume, kernel, (stride, stride, stride), ((0, 0...  33.3 us
    all_gather x1, waiting for transfers between devices, per_device(): first = lax.all_gather(first_filters, 'af', axis=3, tiled=True)  27 us
    all_gather x1, waiting for transfers between devices, per_device(): second = lax.all_gather(second_filters, 'af', axis=3, tiled=True)  15.9 us
    all_to_all x1, blocking collectives, per_device(): lax.all_to_all(features, 'af', split_axis=4, concat_axis=2, tiled=True)  9.29 us
    unnamed x8, local copies, waits for them, and re-layouts  6.65 us
    ppermute x2, waiting for transfers between devices, extended(): lax.ppermute(lax.slice_in_dim(block, 0, high_width, axis=dim), axis, back...  6.24 us
    ppermute x2, starting transfers between devices, extended(): lax.ppermute(lax.slice_in_dim(block, size - low_width, None, axis=dim), a...  6.16 us
    all_to_all x1, local copies, waits for them, and re-layouts, per_device(): lax.all_to_all(features, 'af', split_axis=4, concat_axis=2, tiled=True)  2.96 us
  transfers between devices with their start and end apart: 6, of which 5 were waited for; matrix products, arithmetic and copies ran while one was open for 25% of the time, Pallas kernels for 0%

profile of v1, /device:TPU:0, one launch (start us, length us, event | category | flops | bytes accessed | tf_op | source)
XLA Modules:
  0.0 129.7 jit_solution(3712885760354962032)
XLA Ops:
  6.5 0.0 copy-start
  6.5 0.0 all-gather.3.cloned.1.call-start
  6.5 0.7 all-gather.3.cloned.1.call-update
  7.3 0.0 all-gather.5.cloned.1.call-start
  7.3 0.7 all-gather.5.cloned.1.call-update
  8.0 0.9 slice.16
  8.9 0.1 copy.28
  9.1 4.8 %collective-permute-start = (bf16[2,2,8,8,256]{4,0,3,2,1:T(2,128)(2,1)S(1)}, bf16[2,2,8,8,256]{4,0,3,2,1:T(2,128)(2,1)S(1)}, u32[]{:S(2)}, u32[]{:S(2)}) collective-permute-start(bf16[2,2,8,8,256]{4,0,3,2,1:T(2,128)(2,1)S(1)} %copy.28), channel_id=1, source_target_pairs={{0,8},{8,16},{16,24},{1,9},{9,17},{17,25},{2,10},{10,18},{18,26},{... | collective-permute-start | bytes 393224 | tf_op jit(solution)/shard_map/ppermute | solution.py:12
  13.9 0.8 slice.17
  14.8 0.1 copy.29
  14.9 1.3 collective-permute-start.1
  16.2 0.5 collective-permute-done
  16.7 0.1 constant_dynamic-update-slice_fusion.2
  16.8 0.0 copy-done
  16.8 1.7 %constant_dynamic-update-slice_fusion.1 = bf16[2,19,8,8,256]{4,0,3,2,1:T(2,128)(2,1)S(1)} fusion(bf16[2,19,8,8,256]{4,0,3,2,1:T(2,128)(2,1)S(1)} %constant_dynamic-update-slice_fusion.2, bf16[2,16,8,8,256]{4,3,2,1,0:T(8,128)(2,1)S(1)} %copy-done), kind=kLoop, calls=%fused_computation.9 | loop fusion | bytes 2097152
  18.5 2.5 %collective-permute-done.1 = bf16[2,1,8,8,256]{4,0,3,2,1:T(2,128)(2,1)S(1)} collective-permute-done((bf16[2,1,8,8,256]{4,0,3,2,1:T(2,128)(2,1)S(1)}, bf16[2,1,8,8,256]{4,0,3,2,1:T(2,128)(2,1)S(1)}, u32[]{:S(2)}, u32[]{:S(2)}) %collective-permute-start.1) | collective-permute-done | bytes 65568 | tf_op jit(solution)/shard_map/ppermute | solution.py:15
  21.0 0.1 constant_dynamic-update-slice_fusion
  21.1 0.3 slice.18
  21.4 1.3 %collective-permute-start.2 = (bf16[2,19,2,8,256]{4,0,3,2,1:T(2,128)(2,1)S(1)}, bf16[2,19,2,8,256]{4,0,3,2,1:T(2,128)(2,1)S(1)}, u32[]{:S(2)}, u32[]{:S(2)}) collective-permute-start(bf16[2,19,2,8,256]{4,0,3,2,1:T(2,128)(2,1)S(1)} %slice.18), channel_id=1, source_target_pairs={{0,1},{1,2},{2,3},{3,4},{4,5},{5,6},{6,7},{8,9},{9,10},{10,11},{11... | collective-permute-start | bytes 933896 | tf_op jit(solution)/shard_map/ppermute | solution.py:12
  22.7 0.1 slice.19
  22.8 1.3 collective-permute-start.3
  24.1 0.1 broadcast_and_fusion
  24.2 3.7 %collective-permute-done.3 = bf16[2,19,1,8,256]{4,0,3,2,1:T(2,128)(2,1)S(1)} collective-permute-done((bf16[2,19,1,8,256]{4,0,3,2,1:T(2,128)(2,1)S(1)}, bf16[2,19,1,8,256]{4,0,3,2,1:T(2,128)(2,1)S(1)}, u32[]{:S(2)}, u32[]{:S(2)}) %collective-permute-start.3) | collective-permute-done | bytes 155680 | tf_op jit(solution)/shard_map/ppermute | solution.py:15
  27.9 0.0 collective-permute-done.2
  27.9 27.0 %all-gather.3.cloned.1.call-done = bf16[3,3,3,256,256]{4,3,2,1,0:T(8,128)(2,1)} async-done(((bf16[3,3,3,32,256]{4,3,2,1,0:T(8,128)(2,1)}), bf16[3,3,3,256,256]{4,3,2,1,0:T(8,128)(2,1)}) %all-gather.3.cloned.1.call-update) | async-done | bytes 3538960 | tf_op jit(solution)/shard_map/all_gather | solution.py:31
  54.9 27.7 %broadcast_select_fusion = bf16[2,17,9,8,256]{4,0,3,2,1:T(2,128)(2,1)S(1)} fusion(pred[17,9]{1,0:T(8,128)(4,1)S(1)} %broadcast_and_fusion, bf16[3,3,3,256,256]{4,3,2,1,0:T(8,128)(2,1)} %all-gather.3.cloned.1.call-done, bf16[2,19,1,8,256]{4,0,3,2,1:T(2,128)(2,1)S(1)} %collective-permute-done.3, ...), kind=kOutput, calls=%fused_computation.1 | convolution fusion | flops 7948406784 | bytes 6504601 | tf_op jit(solution)/shard_map/conv_general_dilated | solution.py:20
  82.6 15.9 %all-gather.5.cloned.1.call-done = bf16[3,3,3,256,256]{4,3,2,1,0:T(8,128)(2,1)} async-done(((bf16[3,3,3,32,256]{4,3,2,1,0:T(8,128)(2,1)}), bf16[3,3,3,256,256]{4,3,2,1,0:T(8,128)(2,1)}) %all-gather.5.cloned.1.call-update) | async-done | bytes 3538960 | tf_op jit(solution)/shard_map/all_gather | solution.py:32
  98.5 5.6 %fusion.5 = bf16[2,8,4,4,256]{4,0,3,2,1:T(2,128)(2,1)S(1)} fusion(bf16[2,17,9,8,256]{4,0,3,2,1:T(2,128)(2,1)S(1)} %broadcast_select_fusion, bf16[3,3,3,256,256]{4,3,2,1,0:T(8,128)(2,1)} %all-gather.5.cloned.1.call-done), kind=kOutput, calls=%fused_computation.15 | convolution fusion | flops 830472192 | bytes 4923392 | tf_op jit(solution)/shard_map/conv_general_dilated | solution.py:20
  104.1 0.1 fusion.3
  104.2 1.8 %copy.22 = bf16[2,8,4,4,256]{1,3,2,0,4:T(4,128)(2,1)S(1)} copy(bf16[2,8,4,4,256]{4,1,3,2,0:T(8,128)(2,1)S(1)} %fusion.3) | data formatting | bytes 262144 | tf_op jit(solution)/shard_map/convert_element_type | solution.py:40
  106.0 2.2 %reshape.50 = bf16[8,2,4096]{2,1,0:T(2,128)(2,1)S(1)} reshape(bf16[256,2,4,4,8]{4,3,2,1,0:T(4,128)(2,1)S(1)} %bitcast.10) | data formatting | bytes 262144
  108.2 9.3 %all_to_all.18 = bf16[8,2,4096]{2,1,0:T(2,128)(2,1)S(1)} all-to-all(bf16[8,2,4096]{2,1,0:T(2,128)(2,1)S(1)} %reshape.50), channel_id=1, replica_groups=mesh['col'=4,'af'=8] {'af'}, dimensions={0} | all-to-all | bytes 262144 | tf_op jit(solution)/shard_map/all_to_all | solution.py:41
  117.5 2.4 %reshape.51 = bf16[256,2,4,4,8]{4,3,2,1,0:T(4,128)(2,1)S(1)} reshape(bf16[8,2,4096]{2,1,0:T(2,128)(2,1)S(1)} %all_to_all.18) | data formatting | bytes 262144
  119.9 3.0 %copy.23 = bf16[2,8,8,4,4,32]{5,4,3,2,1,0:T(4,128)(2,1)} copy(bf16[2,8,8,4,4,32]{1,4,3,0,5,2:T(4,128)(2,1)S(1)} %bitcast.9) | data formatting | bytes 262144 | tf_op jit(solution)/shard_map/all_to_all | solution.py:41
  (2 shorter events, 0.0 us)
Async XLA Ops:
  6.5 10.2 %copy-start = (bf16[2,16,8,8,256]{4,3,2,1,0:T(8,128)(2,1)S(1)}, bf16[2,16,8,8,256]{4,3,2,1,0:T(8,128)(2,1)}, u32[]{:S(2)}) copy-start(bf16[2,16,8,8,256]{4,3,2,1,0:T(8,128)(2,1)} %param.3) | copy-start | bytes 3145732
  6.5 48.3 %all-gather.3.cloned.1.call-start = ((), (), s32[]{:S(2)}) async-start(), calls=%async_computation.1 | async-start | bytes 3981312 | tf_op jit(solution)/shard_map/all_gather | solution.py:31
  7.3 91.2 %all-gather.5.cloned.1.call-start = ((), (), s32[]{:S(2)}) async-start(), calls=%async_computation.2 | async-start | bytes 3981312 | tf_op jit(solution)/shard_map/all_gather | solution.py:32
  9.1 7.6 %collective-permute-start = (bf16[2,2,8,8,256]{4,0,3,2,1:T(2,128)(2,1)S(1)}, bf16[2,2,8,8,256]{4,0,3,2,1:T(2,128)(2,1)S(1)}, u32[]{:S(2)}, u32[]{:S(2)}) collective-permute-start(bf16[2,2,8,8,256]{4,0,3,2,1:T(2,128)(2,1)S(1)} %copy.28), channel_id=1, source_target_pairs={{0,8},{8,16},{16,24},{1,9},{9,17},{17,25},{2,10},{10,18},{18,26},{... | collective-permute-start | bytes 393224 | tf_op jit(solution)/shard_map/ppermute | solution.py:12
  14.9 6.2 %collective-permute-start.1 = (bf16[2,1,8,8,256]{4,0,3,2,1:T(2,128)(2,1)S(1)}, bf16[2,1,8,8,256]{4,0,3,2,1:T(2,128)(2,1)S(1)}, u32[]{:S(2)}, u32[]{:S(2)}) collective-permute-start(bf16[2,1,8,8,256]{4,0,3,2,1:T(2,128)(2,1)S(1)} %copy.29), channel_id=1, source_target_pairs={{8,0},{16,8},{24,16},{9,1},{17,9},{25,17},{10,2},{18,10},{26,18},{... | collective-permute-start | bytes 196616 | tf_op jit(solution)/shard_map/ppermute | solution.py:15
  21.4 6.5 %collective-permute-start.2 = (bf16[2,19,2,8,256]{4,0,3,2,1:T(2,128)(2,1)S(1)}, bf16[2,19,2,8,256]{4,0,3,2,1:T(2,128)(2,1)S(1)}, u32[]{:S(2)}, u32[]{:S(2)}) collective-permute-start(bf16[2,19,2,8,256]{4,0,3,2,1:T(2,128)(2,1)S(1)} %slice.18), channel_id=1, source_target_pairs={{0,1},{1,2},{2,3},{3,4},{4,5},{5,6},{6,7},{8,9},{9,10},{10,11},{11... | collective-permute-start | bytes 933896 | tf_op jit(solution)/shard_map/ppermute | solution.py:12
  22.8 5.1 %collective-permute-start.3 = (bf16[2,19,1,8,256]{4,0,3,2,1:T(2,128)(2,1)S(1)}, bf16[2,19,1,8,256]{4,0,3,2,1:T(2,128)(2,1)S(1)}, u32[]{:S(2)}, u32[]{:S(2)}) collective-permute-start(bf16[2,19,1,8,256]{4,0,3,2,1:T(2,128)(2,1)S(1)} %slice.19), channel_id=1, source_target_pairs={{1,0},{2,1},{3,2},{4,3},{5,4},{6,5},{7,6},{9,8},{10,9},{11,10},{12... | collective-permute-start | bytes 466952 | tf_op jit(solution)/shard_map/ppermute | solution.py:15
Sparse Core Ops, SparseCore 0:
  9.0 45.8 all-gather.2
  56.5 41.9 all-gather.4

commit v2 on v1

--- a/solution.py
+++ b/solution.py
@@ -1,7 +1,322 @@
+import functools
+
 import jax
 import jax.numpy as jnp
 from jax import lax
+from jax.experimental import pallas as pl
+from jax.experimental.pallas import tpu as pltpu
 from jax.sharding import PartitionSpec as P
+
+MESH = pl.DeviceIdType.MESH
+
+
+def shifted_three(block, where_inside):
+    w = lax.broadcasted_iota(jnp.int32, block.shape, 1)
+    block = jnp.where(where_inside, block, 0.0)
+    before = jnp.where(w == 0, 0.0, pltpu.roll(block, 1, 1))
+    after = jnp.where(w == block.shape[1] - 1, 0.0, pltpu.roll(block, block.shape[1] - 1, 1))
+    return before, block, after
+
+
+def kernel(
+    cols, rows_count,
+    x_ref, first_ref, second_ref, out_ref,
+    raw, taps_in, hidden, total, sums, packed, w_first, w_second,
+    halo_send, halo_recv, local_sem,
+    z_send, z_recv, xy_send, xy_recv, core_send, core_recv,
+    out_send, out_recv,
+):
+    samples, depth, high, wid, chans = x_ref.shape
+    shard = first_ref.shape[1]
+    c = lax.axis_index("col")
+    k = lax.axis_index("af")
+    z, core = k // 2, lax.rem(k, 2)
+    chips = rows_count // 2
+    planes, lines = depth + 3, high + 3
+
+    def at_col(e):
+        return lax.rem(c + e + cols, cols)
+
+    def at_row(e):
+        return lax.rem(k + e + rows_count, rows_count)
+
+    around = [(dc, dk) for dc in (-1, 0, 1) for dk in (-1, 0, 1) if (dc, dk) != (0, 0)]
+    partners = [(c, at_row(e)) for e in range(1, rows_count)]
+    partners += [(at_col(e), k) for e in range(1, cols)]
+    partners += [(at_col(dc), at_row(dk)) for dc in (-1, 1) for dk in (-1, 1)]
+    barrier = pltpu.get_barrier_semaphore()
+    for partner in partners:
+        pl.semaphore_signal(barrier, inc=1, device_id=partner, device_id_type=MESH)
+    pl.semaphore_wait(barrier, len(partners))
+
+    def remote(src, dst, send, recv, target):
+        return pltpu.make_async_remote_copy(
+            src_ref=src, dst_ref=dst, send_sem=send, recv_sem=recv,
+            device_id=target, device_id_type=MESH,
+        )
+
+    def span(move, size):
+        if move == 1:
+            return pl.ds(size - 2, 2), pl.ds(0, 2)
+        if move == -1:
+            return pl.ds(0, 1), pl.ds(size + 2, 1)
+        return pl.ds(0, size), pl.ds(2, size)
+
+    pending = []
+    other = (c, k + 1 - 2 * core)
+
+    def rows_of(owner):
+        return pl.ds(pl.multiple_of(owner * shard, shard), shard)
+
+    half = shard // 2
+    wide = chans // 2
+
+    def quarter(gathered, owner, part):
+        top = pl.multiple_of(owner * shard + (part // 2) * half, half)
+        left = pl.multiple_of(lax.rem(part, 2) * wide, wide)
+        return gathered.at[:, pl.ds(top, half), pl.ds(left, wide)]
+
+    def own_quarter(source):
+        top = pl.multiple_of((c // 2) * half, half)
+        left = pl.multiple_of(lax.rem(c, 2) * wide, wide)
+        return source.at[:, pl.ds(top, half), pl.ds(left, wide)]
+
+    def begin_gather(n, source, gathered):
+        for r in range(1, chips):
+            target = (c, 2 * lax.rem(z + r, chips) + core)
+            copy = remote(
+                own_quarter(source), quarter(gathered, k, c),
+                z_send.at[n, r - 1], z_recv.at[n, r - 1], target,
+            )
+            copy.start()
+            pending.append(copy)
+        mine = gathered.at[:, rows_of(k), :]
+        copy = remote(source, mine, core_send.at[n, 0], core_recv.at[n, 0], other)
+        copy.start()
+        pending.append(copy)
+
+    def owner_behind(r):
+        return 2 * lax.rem(z - r + chips, chips) + core
+
+    def pass_z(n, gathered):
+        for r in range(1, chips):
+            piece = quarter(gathered, owner_behind(r), c)
+            remote(piece, piece, z_send.at[n, r - 1], z_recv.at[n, r - 1], other).wait_recv()
+            for e in range(1, cols):
+                copy = remote(
+                    piece, piece, xy_send.at[n, r - 1, e - 1], xy_recv.at[n, r - 1, e - 1],
+                    (at_col(e), k),
+                )
+                copy.start()
+                pending.append(copy)
+            copy = remote(piece, piece, core_send.at[n, r], core_recv.at[n, r], other)
+            copy.start()
+            pending.append(copy)
+
+    def pass_xy(n, gathered):
+        for r in range(1, chips):
+            for e in range(1, cols):
+                piece = quarter(gathered, owner_behind(r), at_col(-e))
+                remote(
+                    piece, piece, xy_send.at[n, r - 1, e - 1], xy_recv.at[n, r - 1, e - 1], other
+                ).wait_recv()
+                slot = chips + (r - 1) * (cols - 1) + e - 1
+                copy = remote(piece, piece, core_send.at[n, slot], core_recv.at[n, slot], other)
+                copy.start()
+                pending.append(copy)
+
+    def end_gather(n, gathered):
+        mine = gathered.at[:, rows_of(k + 1 - 2 * core), :]
+        remote(mine, mine, core_send.at[n, 0], core_recv.at[n, 0], other).wait_recv()
+        for slot in range(1, chips + (chips - 1) * (cols - 1)):
+            piece = quarter(gathered, k, c)
+            remote(piece, piece, core_send.at[n, slot], core_recv.at[n, slot], other).wait_recv()
+
+    begin_gather(0, first_ref, w_first)
+    halos = []
+    for i, (dc, dk) in enumerate(around):
+        d_from, d_to = span(dc, depth)
+        h_from, h_to = span(dk, high)
+        copy = remote(
+            x_ref.at[:, d_from, h_from], raw.at[:, d_to, h_to],
+            halo_send.at[i], halo_recv.at[i], (at_col(dc), at_row(dk)),
+        )
+        copy.start()
+        halos.append(copy)
+    own = pltpu.make_async_copy(
+        x_ref, raw.at[:, pl.ds(2, depth), pl.ds(2, high)], local_sem.at[0]
+    )
+    own.start()
+    own_first = pltpu.make_async_copy(first_ref, w_first.at[:, rows_of(k), :], local_sem.at[1])
+    own_second = pltpu.make_async_copy(second_ref, w_second.at[:, rows_of(k), :], local_sem.at[2])
+    own_first.start()
+    own_second.start()
+    pass_z(0, w_first)
+    begin_gather(1, second_ref, w_second)
+    own.wait()
+    for copy in halos:
+        copy.wait()
+
+    def prepare(d, carry):
+        at_depth = c * depth + d - 2
+        line = lax.broadcasted_iota(jnp.int32, (lines, wid, chans), 0) + k * high - 2
+        inside = (
+            (line >= 0) & (line < rows_count * high)
+            & (at_depth >= 0) & (at_depth < cols * depth)
+        )
+        parts = [shifted_three(raw[s, d].astype(jnp.float32), inside) for s in range(samples)]
+        for tap in range(3):
+            both = jnp.concatenate([part[tap] for part in parts], axis=1)
+            taps_in[d, :, :, tap * chans:(tap + 1) * chans] = both.astype(jnp.bfloat16)
+        return carry
+
+    lax.fori_loop(0, planes, prepare, 0)
+    pass_xy(0, w_first)
+    own_first.wait()
+    end_gather(0, w_first)
+    pass_z(1, w_second)
+
+    deep, tall, cells = depth + 1, high + 1, samples * wid
+    step = 3
+
+    def first_tap(t, carry):
+        a, b = t // 3, lax.rem(t, 3)
+        weights = w_first[pl.ds(3 * t, 3)].reshape(3 * chans, chans)
+        for j in range(tall // step):
+            block = taps_in[pl.ds(a, deep), pl.ds(b + step * j, step)]
+            product = jnp.dot(
+                block.reshape(deep * step * cells, 3 * chans), weights,
+                preferred_element_type=jnp.float32,
+            ).reshape(deep, step, cells, chans)
+            at = (slice(None), pl.ds(step * j, step))
+
+            @pl.when(t == 0)
+            def _():
+                total[at] = product
+
+            @pl.when(t > 0)
+            def _():
+                total[at] += product
+
+        return carry
+
+    lax.fori_loop(0, 9, first_tap, 0)
+    pass_xy(1, w_second)
+
+    def activate(d, carry):
+        value = jnp.maximum(total[d], 0.0).reshape(tall * samples, wid, chans)
+        line = lax.broadcasted_iota(jnp.int32, value.shape, 0) // samples
+        inside = (line + k > 0) & (d + c > 0)
+        for tap, part in enumerate(shifted_three(value, inside)):
+            hidden[d, :, :, tap * chans:(tap + 1) * chans] = (
+                part.reshape(tall, cells, chans).astype(jnp.bfloat16)
+            )
+        return carry
+
+    lax.fori_loop(0, deep, activate, 0)
+    own_second.wait()
+    end_gather(1, w_second)
+
+    d_out, h_out = depth // 2, high // 2
+    sums[...] = jnp.zeros_like(sums)
+
+    def second_tap(t, carry):
+        a, b = t // 3, lax.rem(t, 3)
+        weights = w_second[pl.ds(3 * t, 3)].reshape(3 * chans, chans)
+        block = jnp.concatenate(
+            [hidden[a + 2 * d, b + 2 * h] for d in range(d_out) for h in range(h_out)], axis=0
+        )
+        product = jnp.dot(block, weights, preferred_element_type=jnp.float32)
+        for side in range(chans // 128):
+            sums[side] += product[:, 128 * side:128 * (side + 1)]
+        return carry
+
+    lax.fori_loop(0, 9, second_tap, 0)
+
+    count = d_out * h_out * cells // 2
+    parts = 128 // (chans // rows_count)
+    each = count // parts
+    lane = lax.broadcasted_iota(jnp.int32, (each, 128), 1) // (chans // rows_count)
+    for side in range(chans // 128):
+        groups = [
+            jnp.maximum(
+                sums[side, pl.ds(2 * each * g, each, stride=2), :],
+                0.0,
+            )
+            for g in range(parts)
+        ]
+        for q in range(parts):
+            mixed = jnp.zeros((each, 128), jnp.float32)
+            for g in range(parts):
+                turn = ((g - q) % parts) * (chans // rows_count)
+                value = pltpu.roll(groups[g], turn, 1) if turn else groups[g]
+                mixed = jnp.where(lane == g, value, mixed)
+            packed[side * parts + q] = mixed.astype(jnp.bfloat16)
+
+    kept = pltpu.make_async_copy(packed.at[k], out_ref.at[k], local_sem.at[3])
+    kept.start()
+    sent = []
+    for r in range(1, rows_count):
+        copy = remote(
+            packed.at[at_row(r)], out_ref.at[k],
+            out_send.at[r - 1], out_recv.at[r - 1], (c, at_row(r)),
+        )
+        copy.start()
+        sent.append(copy)
+    for copy in pending:
+        copy.wait_send()
+    kept.wait()
+    for copy in sent:
+        copy.wait()
+
+
+def fused(inputs, first_filters, second_filters):
+    cols, rows_count = lax.axis_size("col"), lax.axis_size("af")
+    samples, depth, high, wid, chans = inputs.shape
+    shard = first_filters.shape[3]
+    planes, lines, cells = depth + 3, high + 3, samples * wid
+    d_out, h_out = depth // 2, high // 2
+    count = d_out * h_out * cells // 2
+    parts = 128 // (chans // rows_count)
+    chips = rows_count // 2
+    dma = pltpu.SemaphoreType.DMA
+    slots = chips + (chips - 1) * (cols - 1)
+    bf16, f32 = jnp.bfloat16, jnp.float32
+    out = pl.pallas_call(
+        functools.partial(kernel, cols, rows_count),
+        out_shape=jax.ShapeDtypeStruct((rows_count, count // parts, 128), bf16),
+        in_specs=[pl.BlockSpec(memory_space=pl.ANY)] * 3,
+        out_specs=pl.BlockSpec(memory_space=pltpu.VMEM),
+        scratch_shapes=[
+            pltpu.VMEM((samples, planes, lines, wid, chans), bf16),
+            pltpu.VMEM((planes, lines, cells, 3 * chans), bf16),
+            pltpu.VMEM((depth + 1, high + 1, cells, 3 * chans), bf16),
+            pltpu.VMEM((depth + 1, high + 1, cells, chans), f32),
+            pltpu.VMEM((chans // 128, d_out * h_out * cells, 128), f32),
+            pltpu.VMEM((rows_count, count // parts, 128), bf16),
+            pltpu.VMEM((27, chans, chans), bf16),
+            pltpu.VMEM((27, chans, chans), bf16),
+            dma((8,)), dma((8,)), dma((4,)),
+            dma((2, chips - 1)), dma((2, chips - 1)),
+            dma((2, chips - 1, cols - 1)), dma((2, chips - 1, cols - 1)),
+            dma((2, slots)), dma((2, slots)),
+            dma((rows_count - 1,)), dma((rows_count - 1,)),
+        ],
+        compiler_params=pltpu.CompilerParams(
+            collective_id=0, has_side_effects=True, vmem_limit_bytes=56 * 1024 * 1024
+        ),
+        cost_estimate=pl.CostEstimate(
+            flops=12 * 10**9, bytes_accessed=16 * 10**6, transcendentals=0
+        ),
+    )(
+        inputs,
+        first_filters.reshape(27, shard, chans),
+        second_filters.reshape(27, shard, chans),
+    )
+    low = d_out // parts
+    out = out.reshape(rows_count, low, h_out, samples, wid // 2, parts, shard)
+    out = out.transpose(3, 5, 1, 0, 2, 4, 6)
+    return out.reshape(samples, d_out, rows_count * h_out, wid // 2, shard)
 
 
 def extended(block, axis, dim, low_width, high_width):
@@ -27,7 +342,7 @@
     )
 
 
-def per_device(inputs, first_filters, second_filters):
+def gathered_whole(inputs, first_filters, second_filters):
     first = lax.all_gather(first_filters, "af", axis=3, tiled=True)
     second = lax.all_gather(second_filters, "af", axis=3, tiled=True)
     block = extended(inputs, "col", 1, 2, 1)
@@ -41,6 +356,17 @@
     return lax.all_to_all(features, "af", split_axis=4, concat_axis=2, tiled=True)
 
 
+def per_device(inputs, first_filters, second_filters):
+    samples, depth, high, wid, chans = inputs.shape
+    shard = first_filters.shape[3]
+    fits = (
+        lax.axis_size("col") == 4 and shard == 32 and chans == 256 and wid == 8
+        and samples == 2 and depth % 8 == 0 and high % 6 == 2
+    )
+    plan = fused if fits else gathered_whole
+    return plan(inputs, first_filters, second_filters)
+
+
 def solution(mesh):
     placed = (
         P(None, "col", "af", None, None),

time: 130 us -> 65.9 us (0.51)
  Pallas kernels: 0 us -> 63.6 us
  waiting for transfers between devices: 51 us -> 0 us
  matrix products: 33.3 us -> 0 us
  between operations: 13.5 us -> 0.02 us
  local copies, waits for them, and re-layouts: 13.6 us -> 2.16 us
  blocking collectives: 9.29 us -> 0 us
  starting transfers between devices: 8.78 us -> 0 us
    pallas_call x0 -> x1, Pallas kernels: none -> 63.6 us  [fused(): pl.pallas_call(functools.partial(kernel, cols, rows_count), out_shape=jax...]
    all_gather x2 -> x0, waiting for transfers between devices: 42.9 us -> none  [the longest x1 27 us: per_device(): first = lax.all_gather(first_filters, 'af', axis=3, tiled=True)]
    conv_general_dilated x2 -> x0, matrix products: 33.3 us -> none  [convolve(): lax.conv_general_dilated(volume, kernel, (stride, stride, stride), ((0, 0...]
    all_to_all x1 -> x0, blocking collectives: 9.29 us -> none  [per_device(): lax.all_to_all(features, 'af', split_axis=4, concat_axis=2, tiled=True)]
    ppermute x4 -> x0, starting transfers between devices: 8.74 us -> none  [the longest x2 6.16 us: extended(): lax.ppermute(lax.slice_in_dim(block, size - low_width, None, axis=dim), a...]
    ppermute x4 -> x0, waiting for transfers between devices: 6.73 us -> none  [the longest x2 6.24 us: extended(): lax.ppermute(lax.slice_in_dim(block, 0, high_width, axis=dim), axis, back...]
    unnamed x8 -> x0, local copies, waits for them, and re-layouts: 6.65 us -> none
    all_to_all x1 -> x0, local copies, waits for them, and re-layouts: 2.96 us -> none  [per_device(): lax.all_to_all(features, 'af', split_axis=4, concat_axis=2, tiled=True)]
  transfers between devices with their start and end apart: 6 -> 0, of which waited for: 5 -> 0; matrix products, arithmetic and copies ran while one was open for 25% -> 0% of each run, Pallas kernels for 0% -> 0%
where the time goes in v2:
time: 65.9 us; the launch traced here: 65.8 us
  Pallas kernels  63.6 us (97%)
  local copies, waits for them, and re-layouts  2.16 us (3%)
    pallas_call x1, Pallas kernels, fused(): pl.pallas_call(functools.partial(kernel, cols, rows_count), out_shape=jax...  63.6 us

profile of v2, /device:TPU:0, one launch (start us, length us, event | category | flops | bytes accessed | tf_op | source)
XLA Modules:
  0.0 65.8 jit_solution(5433057498511664206)
XLA Ops:
  0.0 63.6 %shard_map.37 = bf16[8,64,128]{2,1,0:T(8,128)(2,1)} custom-call(bf16[2,16,8,8,256]{4,3,2,1,0:T(8,128)(2,1)} %x_ref.1, bf16[27,32,256]{2,1,0:T(8,128)(2,1)} %bitcast.5, bf16[27,32,256]{2,1,0:T(8,128)(2,1)} %bitcast.6), custom_call_target="tpu_custom_call" | custom-call | flops 12000000000 | bytes 16000000 | tf_op jit(solution)/shard_map/pallas_call | solution.py:285
  63.6 1.1 %reshape.14 = bf16[8,2,4,2,4,4,32]{6,5,4,3,2,1,0:T(4,128)(2,1)S(1)} reshape(bf16[8,64,128]{2,1,0:T(8,128)(2,1)} %shard_map.37) | data formatting | bytes 262144 | tf_op jit(solution)/shard_map/reshape | solution.py:317
  64.7 1.0 %copy.4 = bf16[2,4,2,8,4,4,32]{6,5,4,3,2,1,0:T(4,128)(2,1)} copy(bf16[2,4,2,8,4,4,32]{6,1,5,0,4,2,3:T(4,128)(2,1)S(1)} %bitcast.4) | data formatting | bytes 262144 | tf_op jit(solution)/shard_map/transpose | solution.py:318

commit v3 on v2

--- a/solution.py
+++ b/solution.py
@@ -132,7 +132,10 @@
             piece = quarter(gathered, k, c)
             remote(piece, piece, core_send.at[n, slot], core_recv.at[n, slot], other).wait_recv()
 
-    begin_gather(0, first_ref, w_first)
+    gathers = [
+        (first_ref.at[pl.ds(9 * a, 9)], w_first.at[pl.ds(9 * a, 9)]) for a in range(3)
+    ]
+    gathers.append((second_ref, w_second))
     halos = []
     for i, (dc, dk) in enumerate(around):
         d_from, d_to = span(dc, depth)
@@ -151,8 +154,12 @@
     own_second = pltpu.make_async_copy(second_ref, w_second.at[:, rows_of(k), :], local_sem.at[2])
     own_first.start()
     own_second.start()
-    pass_z(0, w_first)
-    begin_gather(1, second_ref, w_second)
+    for n in range(3):
+        begin_gather(n, *gathers[n])
+    pass_z(0, gathers[0][1])
+    pass_z(1, gathers[1][1])
+    pass_z(2, gathers[2][1])
+    begin_gather(3, *gathers[3])
     own.wait()
     for copy in halos:
         copy.wait()
@@ -171,37 +178,43 @@
         return carry
 
     lax.fori_loop(0, planes, prepare, 0)
-    pass_xy(0, w_first)
     own_first.wait()
-    end_gather(0, w_first)
-    pass_z(1, w_second)
+    pass_xy(0, gathers[0][1])
+    end_gather(0, gathers[0][1])
 
     deep, tall, cells = depth + 1, high + 1, samples * wid
     step = 3
 
-    def first_tap(t, carry):
-        a, b = t // 3, lax.rem(t, 3)
-        weights = w_first[pl.ds(3 * t, 3)].reshape(3 * chans, chans)
+    def first_layer(a):
+        weights = w_first[pl.ds(9 * a, 9)].reshape(9 * chans, chans)
         for j in range(tall // step):
-            block = taps_in[pl.ds(a, deep), pl.ds(b + step * j, step)]
-            product = jnp.dot(
-                block.reshape(deep * step * cells, 3 * chans), weights,
-                preferred_element_type=jnp.float32,
-            ).reshape(deep, step, cells, chans)
+            block = jnp.concatenate(
+                [
+                    taps_in[pl.ds(a, deep), pl.ds(b + step * j, step)].reshape(
+                        deep * step * cells, 3 * chans
+                    )
+                    for b in range(3)
+                ],
+                axis=1,
+            )
+            product = jnp.dot(block, weights, preferred_element_type=jnp.float32).reshape(
+                deep, step, cells, chans
+            )
             at = (slice(None), pl.ds(step * j, step))
-
-            @pl.when(t == 0)
-            def _():
+            if a == 0:
                 total[at] = product
-
-            @pl.when(t > 0)
-            def _():
+            else:
                 total[at] += product
 
-        return carry
-
-    lax.fori_loop(0, 9, first_tap, 0)
-    pass_xy(1, w_second)
+    first_layer(0)
+    pass_xy(1, gathers[1][1])
+    end_gather(1, gathers[1][1])
+    pass_z(3, w_second)
+    first_layer(1)
+    pass_xy(2, gathers[2][1])
+    end_gather(2, gathers[2][1])
+    first_layer(2)
+    pass_xy(3, w_second)
 
     def activate(d, carry):
         value = jnp.maximum(total[d], 0.0).reshape(tall * samples, wid, chans)
@@ -215,23 +228,26 @@
 
     lax.fori_loop(0, deep, activate, 0)
     own_second.wait()
-    end_gather(1, w_second)
+    end_gather(3, w_second)
 
     d_out, h_out = depth // 2, high // 2
-    sums[...] = jnp.zeros_like(sums)
-
-    def second_tap(t, carry):
-        a, b = t // 3, lax.rem(t, 3)
-        weights = w_second[pl.ds(3 * t, 3)].reshape(3 * chans, chans)
+    product = None
+    for a in range(3):
         block = jnp.concatenate(
-            [hidden[a + 2 * d, b + 2 * h] for d in range(d_out) for h in range(h_out)], axis=0
-        )
-        product = jnp.dot(block, weights, preferred_element_type=jnp.float32)
-        for side in range(chans // 128):
-            sums[side] += product[:, 128 * side:128 * (side + 1)]
-        return carry
-
-    lax.fori_loop(0, 9, second_tap, 0)
+            [
+                jnp.concatenate(
+                    [hidden[a + 2 * d, b + 2 * h] for d in range(d_out) for h in range(h_out)],
+                    axis=0,
+                )
+                for b in range(3)
+            ],
+            axis=1,
+        )
+        weights = w_second[pl.ds(9 * a, 9)].reshape(9 * chans, chans)
+        term = jnp.dot(block, weights, preferred_element_type=jnp.float32)
+        product = term if a == 0 else product + term
+    for side in range(chans // 128):
+        sums[side] = product[:, 128 * side:128 * (side + 1)]
 
     count = d_out * h_out * cells // 2
     parts = 128 // (chans // rows_count)
@@ -297,9 +313,9 @@
             pltpu.VMEM((27, chans, chans), bf16),
             pltpu.VMEM((27, chans, chans), bf16),
             dma((8,)), dma((8,)), dma((4,)),
-            dma((2, chips - 1)), dma((2, chips - 1)),
-            dma((2, chips - 1, cols - 1)), dma((2, chips - 1, cols - 1)),
-            dma((2, slots)), dma((2, slots)),
+            dma((4, chips - 1)), dma((4, chips - 1)),
+            dma((4, chips - 1, cols - 1)), dma((4, chips - 1, cols - 1)),
+            dma((4, slots)), dma((4, slots)),
             dma((rows_count - 1,)), dma((rows_count - 1,)),
         ],
         compiler_params=pltpu.CompilerParams(

time: 65.9 us -> 61.3 us (0.930)
  Pallas kernels: 63.6 us -> 59 us
    pallas_call x1, Pallas kernels: 63.6 us -> 59 us  [fused(): pl.pallas_call(functools.partial(kernel, cols, rows_count), out_shape=jax...]
where the time goes in v3:
time: 61.3 us; the launch traced here: 61.2 us
  Pallas kernels  59 us (96%)
  local copies, waits for them, and re-layouts  2.16 us (4%)
    pallas_call x1, Pallas kernels, fused(): pl.pallas_call(functools.partial(kernel, cols, rows_count), out_shape=jax...  59 us

profile of v3, /device:TPU:0, one launch (start us, length us, event | category | flops | bytes accessed | tf_op | source)
XLA Modules:
  0.0 61.2 jit_solution(11572946240275187306)
XLA Ops:
  0.0 59.0 %shard_map.37 = bf16[8,64,128]{2,1,0:T(8,128)(2,1)} custom-call(bf16[2,16,8,8,256]{4,3,2,1,0:T(8,128)(2,1)} %x_ref.1, bf16[27,32,256]{2,1,0:T(8,128)(2,1)} %bitcast.5, bf16[27,32,256]{2,1,0:T(8,128)(2,1)} %bitcast.6), custom_call_target="tpu_custom_call" | custom-call | flops 12000000000 | bytes 16000000 | tf_op jit(solution)/shard_map/pallas_call | solution.py:301
  59.0 1.1 %reshape.14 = bf16[8,2,4,2,4,4,32]{6,5,4,3,2,1,0:T(4,128)(2,1)S(1)} reshape(bf16[8,64,128]{2,1,0:T(8,128)(2,1)} %shard_map.37) | data formatting | bytes 262144 | tf_op jit(solution)/shard_map/reshape | solution.py:333
  60.1 1.0 %copy.4 = bf16[2,4,2,8,4,4,32]{6,5,4,3,2,1,0:T(4,128)(2,1)} copy(bf16[2,4,2,8,4,4,32]{6,1,5,0,4,2,3:T(4,128)(2,1)S(1)} %bitcast.4) | data formatting | bytes 262144 | tf_op jit(solution)/shard_map/transpose | solution.py:334

commit v4 on v3

--- a/solution.py
+++ b/solution.py
@@ -146,6 +146,8 @@
         )
         copy.start()
         halos.append(copy)
+    for n in range(3):
+        begin_gather(n, *gathers[n])
     own = pltpu.make_async_copy(
         x_ref, raw.at[:, pl.ds(2, depth), pl.ds(2, high)], local_sem.at[0]
     )
@@ -154,12 +156,7 @@
     own_second = pltpu.make_async_copy(second_ref, w_second.at[:, rows_of(k), :], local_sem.at[2])
     own_first.start()
     own_second.start()
-    for n in range(3):
-        begin_gather(n, *gathers[n])
     pass_z(0, gathers[0][1])
-    pass_z(1, gathers[1][1])
-    pass_z(2, gathers[2][1])
-    begin_gather(3, *gathers[3])
     own.wait()
     for copy in halos:
         copy.wait()
@@ -177,15 +174,19 @@
             taps_in[d, :, :, tap * chans:(tap + 1) * chans] = both.astype(jnp.bfloat16)
         return carry
 
-    lax.fori_loop(0, planes, prepare, 0)
+    lax.fori_loop(0, planes // 2, prepare, 0)
+    pass_z(1, gathers[1][1])
+    lax.fori_loop(planes // 2, planes, prepare, 0)
     own_first.wait()
     pass_xy(0, gathers[0][1])
+    pass_z(2, gathers[2][1])
+    begin_gather(3, *gathers[3])
     end_gather(0, gathers[0][1])
 
     deep, tall, cells = depth + 1, high + 1, samples * wid
     step = 3
 
-    def first_layer(a):
+    def first_layer(a, following):
         weights = w_first[pl.ds(9 * a, 9)].reshape(9 * chans, chans)
         for j in range(tall // step):
             block = jnp.concatenate(
@@ -205,16 +206,15 @@
                 total[at] = product
             else:
                 total[at] += product
-
-    first_layer(0)
-    pass_xy(1, gathers[1][1])
+            if j == tall // step - 2:
+                pass_xy(following, gathers[following][1])
+
+    first_layer(0, 1)
     end_gather(1, gathers[1][1])
     pass_z(3, w_second)
-    first_layer(1)
-    pass_xy(2, gathers[2][1])
+    first_layer(1, 2)
     end_gather(2, gathers[2][1])
-    first_layer(2)
-    pass_xy(3, w_second)
+    first_layer(2, 3)
 
     def activate(d, carry):
         value = jnp.maximum(total[d], 0.0).reshape(tall * samples, wid, chans)
@@ -376,7 +376,7 @@
     samples, depth, high, wid, chans = inputs.shape
     shard = first_filters.shape[3]
     fits = (
-        lax.axis_size("col") == 4 and shard == 32 and chans == 256 and wid == 8
+        lax.axis_size("col") == 4 and shard == 32 and chans == 256 and wid == 8 and high >= 8
         and samples == 2 and depth % 8 == 0 and high % 6 == 2
     )
     plan = fused if fits else gathered_whole

time: 61.3 us -> 63.1 us (1.029)
  Pallas kernels: 59 us -> 60.7 us
    pallas_call x1, Pallas kernels: 59 us -> 60.7 us  [fused(): pl.pallas_call(functools.partial(kernel, cols, rows_count), out_shape=jax...]
where the time goes in v4:
time: 63.1 us; the launch traced here: 62.9 us
  Pallas kernels  60.7 us (96%)
  local copies, waits for them, and re-layouts  2.16 us (3%)
    pallas_call x1, Pallas kernels, fused(): pl.pallas_call(functools.partial(kernel, cols, rows_count), out_shape=jax...  60.7 us

profile of v4, /device:TPU:0, one launch (start us, length us, event | category | flops | bytes accessed | tf_op | source)
XLA Modules:
  0.0 62.9 jit_solution(1846351813160739686)
XLA Ops:
  0.0 60.7 %shard_map.37 = bf16[8,64,128]{2,1,0:T(8,128)(2,1)} custom-call(bf16[2,16,8,8,256]{4,3,2,1,0:T(8,128)(2,1)} %x_ref.1, bf16[27,32,256]{2,1,0:T(8,128)(2,1)} %bitcast.5, bf16[27,32,256]{2,1,0:T(8,128)(2,1)} %bitcast.6), custom_call_target="tpu_custom_call" | custom-call | flops 12000000000 | bytes 16000000 | tf_op jit(solution)/shard_map/pallas_call | solution.py:301
  60.7 1.1 %reshape.14 = bf16[8,2,4,2,4,4,32]{6,5,4,3,2,1,0:T(4,128)(2,1)S(1)} reshape(bf16[8,64,128]{2,1,0:T(8,128)(2,1)} %shard_map.37) | data formatting | bytes 262144 | tf_op jit(solution)/shard_map/reshape | solution.py:333
  61.9 1.0 %copy.4 = bf16[2,4,2,8,4,4,32]{6,5,4,3,2,1,0:T(4,128)(2,1)} copy(bf16[2,4,2,8,4,4,32]{6,1,5,0,4,2,3:T(4,128)(2,1)S(1)} %bitcast.4) | data formatting | bytes 262144 | tf_op jit(solution)/shard_map/transpose | solution.py:334
